TPU v7x, 256 devices: a whole 4x4x8 slice. The times are simulated.
256 devices in a mesh: sector: 8 (over z), rows: 32 (over x, y, core).
Axes of the slice: x: 4, y: 4, z: 8, core: 2. Of those that a mesh axis runs over, the one named last changes fastest.
Arguments:
- x_block: bfloat16 [8, 40960, 300], P('sector', 'rows')
- h_diag: bfloat16 [8, 40960, 1280], P('sector', 'rows')
- h_right: bfloat16 [8, 40960, 1280], P('sector', 'rows')
- pattern: int32 [8, 2, 320, 10], P('sector', None, 'rows'), may hold values from 0 to 1, as said below
Outputs:
- q_block: bfloat16 [8, 40960, 300], P('sector', 'rows')
- hproj: float32 [8, 300, 300], P('sector')
- correlation: float32 [8, 300, 300], P('sector')
Inputs may be any that keep to these rules, and one draw needn't show every extreme that they name: Within each 1280 x 1280 tile, pattern[s, 0] is symmetric with ones on its diagonal; h_diag's tiles are symmetric.
All inputs are finite; a program needn't handle non-finite values.
Results may differ from a plain program's by a relative error of at most 0.011.
Values may be sent and summed in bfloat16 or wider, within the bound.
A program may use at most 64 MiB of HBM per device.

v0:
```python
import jax
import jax.numpy as jnp
from jax import lax
from jax.sharding import PartitionSpec as P

SUBBLOCK = 128


def from_behind(value, axis, steps):
    count = lax.axis_size(axis)
    leading, last = (max(0, -steps), min(count, count - steps))
    return lax.ppermute(value, axis, [(source, source + steps) for source in range(leading, last)])


def column_product(left, right):
    return lax.dot_general(
        left, right, (((0,), (0,)), ((), ())), preferred_element_type=jnp.float32
    )


def expand(blocks):
    return jnp.repeat(jnp.repeat(blocks, SUBBLOCK, axis=0), SUBBLOCK, axis=1)


def apply_factor(rows_b, inverse):
    return jnp.dot(rows_b.astype(jnp.float32), inverse.T, precision=lax.Precision.HIGH).astype(
        jnp.bfloat16
    )


def shards(x_block, h_diag, h_right, pattern):
    inputs = x_block[0]
    masks = pattern[0].astype(jnp.bfloat16)
    diag_tile = h_diag[0] * expand(masks[0])
    right_tile = h_right[0] * expand(masks[1])
    later_rows = from_behind(inputs, "rows", -1)
    carried = column_product(right_tile, inputs)
    earlier = from_behind(carried.astype(jnp.bfloat16), "rows", 1).astype(carried.dtype)
    image = jnp.dot(diag_tile, inputs, preferred_element_type=jnp.float32)
    image = image + jnp.dot(right_tile, later_rows, preferred_element_type=jnp.float32) + earlier
    image_b = image.astype(jnp.bfloat16)
    total_rows = lax.axis_size("rows") * inputs.shape[0]
    gram, rayleigh = lax.psum(
        (column_product(image_b, image_b), column_product(inputs, image_b)), "rows"
    )
    gram = gram / total_rows
    rayleigh = rayleigh / total_rows
    factor = jnp.linalg.cholesky(gram)
    inverse = jax.scipy.linalg.solve_triangular(
        factor, jnp.eye(gram.shape[0], dtype=jnp.float32), lower=True
    )
    basis = apply_factor(image_b, inverse)
    previous = from_behind(basis, "sector", 1)
    correlation = (
        lax.psum(column_product(previous, basis).astype(jnp.bfloat16), "rows").astype(jnp.float32)
        / total_rows
    )
    return (basis[None], rayleigh[None], correlation[None])


def solution(mesh):
    in_specs = (
        P("sector", "rows", None),
        P("sector", "rows", None),
        P("sector", "rows", None),
        P("sector", None, "rows", None),
    )
    out_specs = (P("sector", "rows", None), P("sector", None, None), P("sector", None, None))
    return jax.shard_map(shards, mesh=mesh, in_specs=in_specs, out_specs=out_specs, check_vma=False)
```

profile of v0, /device:TPU:1, one launch (start us, length us, event | category | flops | bytes accessed | tf_op | source)
XLA Modules:
  0.0 392.8 jit_solution(5937771413376753806)
XLA Ops:
  7.2 0.0 all-reduce.9.cloned.1.call-start
  7.2 0.7 copy_convert_fusion
  7.9 0.1 copy.17
  8.0 0.1 broadcast_bitcast_fusion
  8.2 4.0 %copy.16 = bf16[1,1280,1280]{1,2,0:T(8,128)(2,1)S(1)} copy(bf16[1,1280,1280]{2,1,0:T(8,128)(2,1)} %param.6) | data formatting | bytes 6553600 | tf_op args[2]
  12.2 0.2 bitcast_multiply_fusion
  12.4 3.2 fusion.6
  15.7 4.6 %collective-permute-start.1 = (bf16[1280,300]{0,1:T(8,128)(2,1)}, bf16[1280,300]{0,1:T(8,128)(2,1)}, u32[]{:S(2)}, u32[]{:S(2)}) collective-permute-start(bf16[1280,300]{0,1:T(8,128)(2,1)} %fusion.6), channel_id=1, source_target_pairs={{0,1},{1,2},{2,3},{3,4},{4,5},{5,6},{6,7},{7,8},{8,9},{9,10},{10,1... | collective-permute-start | bytes 2304008 | tf_op jit(solution)/shard_map/ppermute | solution.py:12
  20.2 2.7 collective-permute-start
  23.0 1.9 bitcast_multiply_fusion.1
  24.9 0.1 copy.14
  25.0 0.1 broadcast_bitcast_fusion.1
  25.1 4.0 %copy.15 = bf16[1,1280,1280]{1,2,0:T(8,128)(2,1)S(1)} copy(bf16[1,1280,1280]{2,1,0:T(8,128)(2,1)} %param.5) | data formatting | bytes 6553600 | tf_op args[1]
  29.2 0.2 bitcast_multiply_fusion.2
  29.4 0.0 copy-start
  29.4 2.5 fusion.2
  31.9 0.0 collective-permute-done.1
  31.9 1.9 collective-permute-done
  33.8 0.0 copy-done
  33.8 2.7 fusion.5
  36.5 2.5 convolution_bitcast_fusion
  39.0 1.4 fusion.39
  40.3 0.0 all-reduce.9.cloned.1.call-update
  40.4 0.2 all-reduce.7.cloned.1.call-start
  40.7 118.3 %all-reduce.9.cloned.1.call-done = (f32[300,300]{0,1:T(8,128)}, f32[300,300]{0,1:T(8,128)}) async-done(((f32[300,300]{0,1:T(8,128)}, f32[300,300]{0,1:T(8,128)}), (f32[300,300]{0,1:T(8,128)}, f32[300,300]{0,1:T(8,128)})) %all-reduce.9.cloned.1.call-update) | async-done | bytes 720016 | tf_op jit(solution)/shard_map/psum | solution.py:43
  159.0 1.1 broadcast_multiply_fusion
  160.1 0.2 copy.20
  160.3 1.1 fusion.14
  161.4 11.7 %cholesky.78 = f32[128,128]{1,0:T(8,128)S(1)} custom-call(f32[128,128]{1,0:T(8,128)S(1)} %cholesky.198), custom_call_target="Cholesky" | custom-call | tf_op jit(solution)/shard_map/jit(cholesky)/cholesky | solution.py:48
  173.2 9.8 %custom-call.23 = f32[1,128,128]{1,2,0:T(8,128)S(1)} custom-call(f32[1,128,128]{2,1,0:T(8,128)S(1)} %get-tuple-element.33), custom_call_target="InvertDiagBlocksLowerTriangular" | custom-call | tf_op jit(solution)/shard_map/jit(cholesky)/cholesky | solution.py:48
  183.0 0.2 constant_dynamic-update-slice_fusion.2
  183.3 0.3 convolution_subtract_fusion.1
  183.5 11.7 %cholesky.164 = f32[128,128]{1,0:T(8,128)S(1)} custom-call(f32[128,128]{1,0:T(8,128)S(1)} %cholesky.202), custom_call_target="Cholesky" | custom-call | tf_op jit(solution)/shard_map/jit(cholesky)/cholesky | solution.py:48
  195.3 10.0 %custom-call.24 = f32[1,128,128]{1,2,0:T(8,128)S(1)} custom-call(f32[1,128,128]{2,1,0:T(8,128)S(1)} %get-tuple-element.30), custom_call_target="InvertDiagBlocksLowerTriangular" | custom-call | tf_op jit(solution)/shard_map/jit(cholesky)/cholesky | solution.py:48
  205.3 0.2 convolution_dynamic-update-slice_fusion
  205.5 0.2 convolution_subtract_fusion.3
  205.7 4.0 %cholesky.186 = f32[44,44]{1,0:T(8,128)S(1)} custom-call(f32[44,44]{1,0:T(8,128)S(1)} %convolution_subtract_fusion.3), custom_call_target="Cholesky" | custom-call | tf_op jit(solution)/shard_map/jit(cholesky)/cholesky | solution.py:48
  209.7 0.6 compare_reduce_fusion
  210.4 0.6 compare_reduce_fusion.1
  213.0 0.1 triangular_solve.99
  213.1 4.0 %while.1 = (s32[]{:T(128)}, f32[300,300]{1,0:T(8,128)S(1)}, s32[2,2]{1,0:T(2,128)S(1)}, f32[2,128,128]{2,1,0:T(8,128)S(1)}, s32[]{:T(128)}) while((s32[]{:T(128)}, f32[300,300]{1,0:T(8,128)S(1)}, s32[2,2]{1,0:T(2,128)S(1)}, f32[2,128,128]{2,1,0:T(8,128)S(1)}, s32[]{:T(128)}) %tuple.32), condition=%wide.while_cond, body=%wide.while_body.sunk | while | flops 2 | bytes 131181 | solution.py:49
  213.1 0.6 fusion.53
  213.7 1.4 bitcast_dynamic-update-slice_fusion.2
  215.1 0.6 fusion.53
  215.7 1.4 bitcast_dynamic-update-slice_fusion.2
  217.1 0.1 fusion.25
  217.2 0.0 copy-start.2
  217.2 29.5 %custom-call.25 = f32[3,128,128]{1,2,0:T(8,128)S(1)} custom-call(f32[3,128,128]{2,1,0:T(8,128)S(1)} %pad_maximum_fusion), custom_call_target="InvertDiagBlocksLowerTriangular" | custom-call | tf_op jit(solution)/shard_map/jit(_solve_triangular)/triangular_solve | solution.py:49
  246.7 0.3 fusion.18
  247.0 0.3 convolution_subtract_fusion
  247.4 0.5 fusion.24
  247.8 0.4 convolution_subtract_fusion.2
  248.3 0.4 fusion.31
  248.7 1.0 convolution_convert_fusion
  249.7 0.0 copy-start.1
  249.8 3.2 collective-permute-start.2
  253.0 16.3 %collective-permute-done.2 = bf16[1280,300]{0,1:T(8,128)(2,1)S(1)} collective-permute-done((bf16[1280,300]{0,1:T(8,128)(2,1)S(1)}, bf16[1280,300]{0,1:T(8,128)(2,1)S(1)}, u32[]{:S(2)}, u32[]{:S(2)}) %collective-permute-start.2) | collective-permute-done | bytes 768032 | tf_op jit(solution)/shard_map/ppermute | solution.py:12
  269.3 1.3 convolution_convert_fusion.1
  270.6 0.0 all-reduce.7.cloned.1.call-update
  270.6 0.0 copy-done.2
  270.7 1.2 copy.22
  271.9 112.0 %all-reduce.7.cloned.1.call-done = bf16[300,300]{0,1:T(8,128)(2,1)} async-done(((bf16[300,300]{0,1:T(8,128)(2,1)}), bf16[300,300]{0,1:T(8,128)(2,1)}) %all-reduce.7.cloned.1.call-update) | async-done | bytes 180016 | tf_op jit(solution)/shard_map/psum | solution.py:55
  383.8 1.0 multiply_bitcast_fusion
  384.8 1.2 copy.23
  (24 shorter events, 0.4 us)
Async XLA Ops:
  7.2 151.9 %all-reduce.9.cloned.1.call-start = ((), (), s32[]{:S(2)}) async-start(), calls=%async_computation.1 | async-start | bytes 1867776 | tf_op jit(solution)/shard_map/psum | solution.py:43
  15.7 16.3 %collective-permute-start.1 = (bf16[1280,300]{0,1:T(8,128)(2,1)}, bf16[1280,300]{0,1:T(8,128)(2,1)}, u32[]{:S(2)}, u32[]{:S(2)}) collective-permute-start(bf16[1280,300]{0,1:T(8,128)(2,1)} %fusion.6), channel_id=1, source_target_pairs={{0,1},{1,2},{2,3},{3,4},{4,5},{5,6},{6,7},{7,8},{8,9},{9,10},{10,1... | collective-permute-start | bytes 2304008 | tf_op jit(solution)/shard_map/ppermute | solution.py:12
  20.2 13.5 %collective-permute-start = (bf16[1280,300]{0,1:T(8,128)(2,1)}, bf16[1280,300]{0,1:T(8,128)(2,1)}, u32[]{:S(2)}, u32[]{:S(2)}) collective-permute-start(bf16[1280,300]{0,1:T(8,128)(2,1)} %bitcast.3), channel_id=1, source_target_pairs={{1,0},{2,1},{3,2},{4,3},{5,4},{6,5},{7,6},{8,7},{9,8},{10,9},{11,1... | collective-permute-start | bytes 2304008 | tf_op jit(solution)/shard_map/ppermute | solution.py:12
  29.4 4.4 %copy-start = (bf16[1280,1280]{0,1:T(8,128)(2,1)S(1)}, bf16[1280,1280]{0,1:T(8,128)(2,1)}, u32[]{:S(2)}) copy-start(bf16[1280,1280]{0,1:T(8,128)(2,1)} %bitcast_multiply_fusion.1) | copy-start | bytes 9830404
  40.4 343.5 %all-reduce.7.cloned.1.call-start = ((), (), s32[]{:S(2)}) async-start(), calls=%async_computation | async-start | bytes 466944 | tf_op jit(solution)/shard_map/psum | solution.py:55
  217.2 53.5 %copy-start.2 = (f32[300,300]{0,1:T(8,128)S(1)}, f32[300,300]{0,1:T(8,128)}, u32[]{:S(2)}) copy-start(f32[300,300]{0,1:T(8,128)} %get-tuple-element.26) | copy-start | bytes 1080004
  249.7 136.2 %copy-start.1 = (bf16[1280,300]{0,1:T(8,128)(2,1)}, bf16[1280,300]{0,1:T(8,128)(2,1)S(1)}, u32[]{:S(2)}) copy-start(bf16[1280,300]{0,1:T(8,128)(2,1)S(1)} %convolution_convert_fusion) | copy-start | bytes 2304004
  249.8 19.6 %collective-permute-start.2 = (bf16[1280,300]{0,1:T(8,128)(2,1)S(1)}, bf16[1280,300]{0,1:T(8,128)(2,1)S(1)}, u32[]{:S(2)}, u32[]{:S(2)}) collective-permute-start(bf16[1280,300]{0,1:T(8,128)(2,1)S(1)} %convolution_convert_fusion), channel_id=1, source_target_pairs={{0,32},{32,64},{64,96},{96,128},{128,160},{160,192},{192,224},{1,3... | collective-permute-start | bytes 2304008 | tf_op jit(solution)/shard_map/ppermute | solution.py:12
Sparse Core Ops, SparseCore 0:
  40.5 118.5 all-reduce.8
  270.7 113.0 all-reduce.6
where the time goes:
time: 393 us
  waiting for transfers between devices  248 us (63%)
  other arithmetic  84.6 us (22%)
  matrix products  17.4 us (4%)
  between operations  16.4 us (4%)
  local copies, waits for them, and re-layouts  15.1 us (4%)
  starting transfers between devices  10.8 us (3%)
    psum x1, waiting for transfers between devices, shards(): lax.psum((column_product(image_b, image_b), column_product(inputs, image_...  118 us
    psum x1, waiting for transfers between devices, shards(): lax.psum(column_product(previous, basis).astype(jnp.bfloat16), 'rows')  112 us
    another operation x10, other arithmetic, shards(): factor = jnp.linalg.cholesky(gram)  48.6 us
    another operation x7, other arithmetic, shards(): jax.scipy.linalg.solve_triangular(factor, jnp.eye(gram.shape[0], dtype=jn...  29.7 us
    ppermute x3, waiting for transfers between devices, from_behind(): lax.ppermute(value, axis, [(source, source + steps) for source in range(l...  18.2 us
    unnamed x16, local copies, waits for them, and re-layouts  10.7 us
    ppermute x3, starting transfers between devices, from_behind(): lax.ppermute(value, axis, [(source, source + steps) for source in range(l...  10.5 us
    dot_general x4, matrix products, column_product(): lax.dot_general(left, right, (((0,), (0,)), ((), ())), preferred_element_...  8.37 us
  transfers between devices with their start and end apart: 5, of which 4 were waited for; matrix products, arithmetic and copies ran while one was open for 3% of the time, Pallas kernels for 0%

commit v1 on v0

--- a/solution.py
+++ b/solution.py
@@ -51,8 +51,12 @@
     )
     basis = apply_factor(image_b, inverse)
     previous = from_behind(basis, "sector", 1)
+
+    def store_core_now(my_tile):
+        return jnp.sum(jax.lax.all_gather(my_tile, "rows"), axis=0)
+
     correlation = (
-        lax.psum(column_product(previous, basis).astype(jnp.bfloat16), "rows").astype(jnp.float32)
+        store_core_now(column_product(previous, basis).astype(jnp.bfloat16)).astype(jnp.float32)
         / total_rows
     )
     return (basis[None], rayleigh[None], correlation[None])

time: 393 us -> 342 us (0.87)
  waiting for transfers between devices: 248 us -> 194 us
    psum x1 -> x0, waiting for transfers between devices: 112 us -> none  [shards(): lax.psum(column_product(previous, basis).astype(jnp.bfloat16), 'rows')]
    all_gather x0 -> x1, waiting for transfers between devices: none -> 57.3 us  [store_core_now(): return jnp.sum(jax.lax.all_gather(my_tile, 'rows'), axis=0)]
    reduce_sum x0 -> x1, other arithmetic: none -> 4.47 us  [store_core_now(): return jnp.sum(jax.lax.all_gather(my_tile, 'rows'), axis=0)]
where the time goes in v1:
time: 342 us; the launch traced here: 341 us
  waiting for transfers between devices  194 us (57%)
  other arithmetic  88.1 us (26%)
  matrix products  16.9 us (5%)
  between operations  16.4 us (5%)
  local copies, waits for them, and re-layouts  15.3 us (4%)
  starting transfers between devices  10.8 us (3%)
    psum x1, waiting for transfers between devices, shards(): lax.psum((column_product(image_b, image_b), column_product(inputs, image_...  118 us
    all_gather x1, waiting for transfers between devices, store_core_now(): return jnp.sum(jax.lax.all_gather(my_tile, 'rows'), axis=0)  57.3 us
    another operation x10, other arithmetic, shards(): factor = jnp.linalg.cholesky(gram)  48.6 us
    another operation x7, other arithmetic, shards(): jax.scipy.linalg.solve_triangular(factor, jnp.eye(gram.shape[0], dtype=jn...  29.7 us
    ppermute x3, waiting for transfers between devices, from_behind(): lax.ppermute(value, axis, [(source, source + steps) for source in range(l...  18.2 us
    unnamed x16, local copies, waits for them, and re-layouts  10.7 us
    ppermute x3, starting transfers between devices, from_behind(): lax.ppermute(value, axis, [(source, source + steps) for source in range(l...  10.5 us
    dot_general x4, matrix products, column_product(): lax.dot_general(left, right, (((0,), (0,)), ((), ())), preferred_element_...  8.37 us
  transfers between devices with their start and end apart: 5, of which 4 were waited for; matrix products, arithmetic and copies ran while one was open for 3% of the time, Pallas kernels for 0%

profile of v1, /device:TPU:1, one launch (start us, length us, event | category | flops | bytes accessed | tf_op | source)
XLA Modules:
  0.0 341.4 jit_solution(3297947666557771156)
XLA Ops:
  7.2 0.0 all-reduce.6.cloned.1.call-start
  7.2 0.7 copy_convert_fusion
  7.9 0.1 copy.26
  8.0 0.1 broadcast_bitcast_fusion
  8.2 4.0 %copy.25 = bf16[1,1280,1280]{1,2,0:T(8,128)(2,1)S(1)} copy(bf16[1,1280,1280]{2,1,0:T(8,128)(2,1)} %param.6) | data formatting | bytes 6553600 | tf_op args[2]
  12.2 0.2 bitcast_multiply_fusion
  12.4 3.2 fusion.6
  15.7 4.6 %collective-permute-start.1 = (bf16[1280,300]{0,1:T(8,128)(2,1)}, bf16[1280,300]{0,1:T(8,128)(2,1)}, u32[]{:S(2)}, u32[]{:S(2)}) collective-permute-start(bf16[1280,300]{0,1:T(8,128)(2,1)} %fusion.6), channel_id=1, source_target_pairs={{0,1},{1,2},{2,3},{3,4},{4,5},{5,6},{6,7},{7,8},{8,9},{9,10},{10,1... | collective-permute-start | bytes 2304008 | tf_op jit(solution)/shard_map/ppermute | solution.py:12
  20.2 2.7 collective-permute-start
  23.0 1.9 bitcast_multiply_fusion.1
  24.9 0.1 copy.23
  25.0 0.1 broadcast_bitcast_fusion.1
  25.1 4.0 %copy.24 = bf16[1,1280,1280]{1,2,0:T(8,128)(2,1)S(1)} copy(bf16[1,1280,1280]{2,1,0:T(8,128)(2,1)} %param.5) | data formatting | bytes 6553600 | tf_op args[1]
  29.2 0.2 bitcast_multiply_fusion.2
  29.4 0.0 copy-start
  29.4 2.5 fusion.2
  31.9 0.0 collective-permute-done.1
  31.9 1.9 collective-permute-done
  33.8 0.0 copy-done
  33.8 2.7 fusion.5
  36.5 2.5 convolution_bitcast_fusion
  39.0 1.4 fusion.40
  40.3 0.0 all-reduce.6.cloned.1.call-update
  40.4 0.2 all-gather.4.cloned.1.call-start
  40.7 118.3 %all-reduce.6.cloned.1.call-done = (f32[300,300]{0,1:T(8,128)}, f32[300,300]{0,1:T(8,128)}) async-done(((f32[300,300]{0,1:T(8,128)}, f32[300,300]{0,1:T(8,128)}), (f32[300,300]{0,1:T(8,128)}, f32[300,300]{0,1:T(8,128)})) %all-reduce.6.cloned.1.call-update) | async-done | bytes 720016 | tf_op jit(solution)/shard_map/psum | solution.py:43
  159.0 1.1 broadcast_multiply_fusion
  160.1 0.2 copy.29
  160.3 1.1 fusion.15
  161.4 11.7 %cholesky.78 = f32[128,128]{1,0:T(8,128)S(1)} custom-call(f32[128,128]{1,0:T(8,128)S(1)} %cholesky.198), custom_call_target="Cholesky" | custom-call | tf_op jit(solution)/shard_map/jit(cholesky)/cholesky | solution.py:48
  173.2 9.8 %custom-call.23 = f32[1,128,128]{1,2,0:T(8,128)S(1)} custom-call(f32[1,128,128]{2,1,0:T(8,128)S(1)} %get-tuple-element.36), custom_call_target="InvertDiagBlocksLowerTriangular" | custom-call | tf_op jit(solution)/shard_map/jit(cholesky)/cholesky | solution.py:48
  183.0 0.2 constant_dynamic-update-slice_fusion.2
  183.3 0.3 convolution_subtract_fusion.2
  183.6 11.7 %cholesky.164 = f32[128,128]{1,0:T(8,128)S(1)} custom-call(f32[128,128]{1,0:T(8,128)S(1)} %cholesky.202), custom_call_target="Cholesky" | custom-call | tf_op jit(solution)/shard_map/jit(cholesky)/cholesky | solution.py:48
  195.3 10.0 %custom-call.24 = f32[1,128,128]{1,2,0:T(8,128)S(1)} custom-call(f32[1,128,128]{2,1,0:T(8,128)S(1)} %get-tuple-element.33), custom_call_target="InvertDiagBlocksLowerTriangular" | custom-call | tf_op jit(solution)/shard_map/jit(cholesky)/cholesky | solution.py:48
  205.3 0.2 convolution_dynamic-update-slice_fusion
  205.5 0.2 convolution_subtract_fusion.3
  205.7 4.0 %cholesky.186 = f32[44,44]{1,0:T(8,128)S(1)} custom-call(f32[44,44]{1,0:T(8,128)S(1)} %convolution_subtract_fusion.3), custom_call_target="Cholesky" | custom-call | tf_op jit(solution)/shard_map/jit(cholesky)/cholesky | solution.py:48
  209.7 0.6 compare_reduce_fusion
  210.4 0.6 compare_reduce_fusion.1
  213.0 0.1 triangular_solve.99
  213.1 4.0 %while.1 = (s32[]{:T(128)}, f32[300,300]{1,0:T(8,128)S(1)}, s32[2,2]{1,0:T(2,128)S(1)}, f32[2,128,128]{2,1,0:T(8,128)S(1)}, s32[]{:T(128)}) while((s32[]{:T(128)}, f32[300,300]{1,0:T(8,128)S(1)}, s32[2,2]{1,0:T(2,128)S(1)}, f32[2,128,128]{2,1,0:T(8,128)S(1)}, s32[]{:T(128)}) %tuple.33), condition=%wide.while_cond, body=%wide.while_body.sunk | while | flops 2 | bytes 131181 | solution.py:49
  213.1 0.6 fusion.54
  213.7 1.4 bitcast_dynamic-update-slice_fusion.2
  215.1 0.6 fusion.54
  215.7 1.4 bitcast_dynamic-update-slice_fusion.2
  217.1 0.1 fusion.26
  217.2 29.5 %custom-call.25 = f32[3,128,128]{1,2,0:T(8,128)S(1)} custom-call(f32[3,128,128]{2,1,0:T(8,128)S(1)} %pad_maximum_fusion), custom_call_target="InvertDiagBlocksLowerTriangular" | custom-call | tf_op jit(solution)/shard_map/jit(_solve_triangular)/triangular_solve | solution.py:49
  246.7 0.2 fusion.19
  246.9 0.3 convolution_subtract_fusion.1
  247.2 0.3 fusion.25
  247.5 0.4 convolution_subtract_fusion
  247.9 0.3 fusion.32
  248.2 1.0 convolution_convert_fusion
  249.2 0.0 copy-start.1
  249.2 3.2 collective-permute-start.2
  252.5 16.3 %collective-permute-done.2 = bf16[1280,300]{0,1:T(8,128)(2,1)S(1)} collective-permute-done((bf16[1280,300]{0,1:T(8,128)(2,1)S(1)}, bf16[1280,300]{0,1:T(8,128)(2,1)S(1)}, u32[]{:S(2)}, u32[]{:S(2)}) %collective-permute-start.2) | collective-permute-done | bytes 768032 | tf_op jit(solution)/shard_map/ppermute | solution.py:12
  268.8 1.3 fusion.9
  270.1 0.0 all-gather.4.cloned.1.call-update
  270.1 0.0 copy-done.2
  270.2 1.2 copy.33
  271.3 57.3 %all-gather.4.cloned.1.call-done = bf16[32,300,300]{2,1,0:T(8,128)(2,1)} async-done(((bf16[1,300,300]{2,1,0:T(8,128)(2,1)}), bf16[32,300,300]{2,1,0:T(8,128)(2,1)}) %all-gather.4.cloned.1.call-update) | async-done | bytes 5760016 | tf_op jit(solution)/shard_map/all_gather | solution.py:56
  328.7 4.5 %reduce_sum.12 = bf16[300,300]{1,0:T(8,128)(2,1)S(1)} reduce(bf16[32,300,300]{2,1,0:T(8,128)(2,1)} %all-gather.4.cloned.1.call-done, bf16[]{:T(256)} %constant.127.clone.1), dimensions={0}, to_apply=%region_8.9 | reduce | flops 2790000 | bytes 5940002 | tf_op jit(solution)/shard_map/reduce_sum | solution.py:56
  333.2 0.2 copy.32
  333.4 1.2 copy.34
  (26 shorter events, 0.5 us)
Async XLA Ops:
  7.2 151.9 %all-reduce.6.cloned.1.call-start = ((), (), s32[]{:S(2)}) async-start(), calls=%async_computation.1 | async-start | bytes 1867776 | tf_op jit(solution)/shard_map/psum | solution.py:43
  15.7 16.3 %collective-permute-start.1 = (bf16[1280,300]{0,1:T(8,128)(2,1)}, bf16[1280,300]{0,1:T(8,128)(2,1)}, u32[]{:S(2)}, u32[]{:S(2)}) collective-permute-start(bf16[1280,300]{0,1:T(8,128)(2,1)} %fusion.6), channel_id=1, source_target_pairs={{0,1},{1,2},{2,3},{3,4},{4,5},{5,6},{6,7},{7,8},{8,9},{9,10},{10,1... | collective-permute-start | bytes 2304008 | tf_op jit(solution)/shard_map/ppermute | solution.py:12
  20.2 13.5 %collective-permute-start = (bf16[1280,300]{0,1:T(8,128)(2,1)}, bf16[1280,300]{0,1:T(8,128)(2,1)}, u32[]{:S(2)}, u32[]{:S(2)}) collective-permute-start(bf16[1280,300]{0,1:T(8,128)(2,1)} %bitcast.3), channel_id=1, source_target_pairs={{1,0},{2,1},{3,2},{4,3},{5,4},{6,5},{7,6},{8,7},{9,8},{10,9},{11,1... | collective-permute-start | bytes 2304008 | tf_op jit(solution)/shard_map/ppermute | solution.py:12
  29.4 4.4 %copy-start = (bf16[1280,1280]{0,1:T(8,128)(2,1)S(1)}, bf16[1280,1280]{0,1:T(8,128)(2,1)}, u32[]{:S(2)}) copy-start(bf16[1280,1280]{0,1:T(8,128)(2,1)} %bitcast_multiply_fusion.1) | copy-start | bytes 9830404
  40.4 288.3 %all-gather.4.cloned.1.call-start = ((), (), s32[]{:S(2)}) async-start(), calls=%async_computation | async-start | bytes 7704576 | tf_op jit(solution)/shard_map/all_gather | solution.py:56
  217.2 52.9 %copy-start.2 = (f32[300,300]{0,1:T(8,128)S(1)}, f32[300,300]{0,1:T(8,128)}, u32[]{:S(2)}) copy-start(f32[300,300]{0,1:T(8,128)} %get-tuple-element.29) | copy-start | bytes 1080004
  249.2 83.9 %copy-start.1 = (bf16[1280,300]{0,1:T(8,128)(2,1)}, bf16[1280,300]{0,1:T(8,128)(2,1)S(1)}, u32[]{:S(2)}) copy-start(bf16[1280,300]{0,1:T(8,128)(2,1)S(1)} %convolution_convert_fusion) | copy-start | bytes 2304004
  249.2 19.6 %collective-permute-start.2 = (bf16[1280,300]{0,1:T(8,128)(2,1)S(1)}, bf16[1280,300]{0,1:T(8,128)(2,1)S(1)}, u32[]{:S(2)}, u32[]{:S(2)}) collective-permute-start(bf16[1280,300]{0,1:T(8,128)(2,1)S(1)} %convolution_convert_fusion), channel_id=1, source_target_pairs={{0,32},{32,64},{64,96},{96,128},{128,160},{160,192},{192,224},{1,3... | collective-permute-start | bytes 2304008 | tf_op jit(solution)/shard_map/ppermute | solution.py:12
Sparse Core Ops, SparseCore 0:
  40.5 118.5 all-reduce.5
  270.2 58.4 all-gather.3
